TPU v7x, 256 devices: a whole 4x4x8 slice. The times are simulated.
256 devices in a mesh: dom: 32 (over z, x), col: 8 (over y, core).
Axes of the slice: x: 4, y: 4, z: 8, core: 2. Of those that a mesh axis runs over, the one named last changes fastest.
Arguments:
- features: bfloat16 [65536, 128], P(('dom', 'col'))
- w_hidden: bfloat16 [128, 256], replicated, may hold values from -0.5 to 0.5
- w_out: bfloat16 [256, 256], replicated, may hold values from -0.375 to 0.375
- block_values: bfloat16 [8192, 4096], P('dom'), may hold values from 0.0009994507 to 1
- block_slot: int32 [8192], P('dom'), may hold values from 0 to 159, as said below
- requested: int32 [32, 32, 4], P('dom'), may hold values from -1 to 31, as said below
- labels: int32 [65536], P('dom'), may hold values from 0 to 171
- train_mask: int32 [65536], P('dom'), may hold values 0 or 1
Outputs:
- propagated: float32 [256, 65536], P('col', 'dom')
- logit_grad: float32 [256, 65536], P('col', 'dom')
Inputs may be any that keep to these rules, and one draw needn't show every extreme that they name: requested[q, p, :] lists distinct row blocks of partition p first and -1 for the rest; it is all -1 for p = q and has at least one entry for every other p; for each q some p has all 4 entries. `block_slot`: each slot s >= 32 that a block of partition q names has requested[q, (s - 32) // 4, (s - 32) % 4] >= 0, and every such entry of requested is named by exactly one block of q; partition 0 reads 4 blocks from the last partition.
All inputs are finite; a program needn't handle non-finite values. No bound on the sum of `train_mask` on one device may be relied on, other than what follows from the above.
Results may differ from a plain program's by a relative error of at most 0.0037.
Values may be sent and summed in bfloat16 or wider, within the bound.
A program may use at most 64 MiB of HBM per device.

v0:
```python
import functools

import jax
import jax.numpy as jnp
from jax import lax
from jax.experimental import pallas as pl
from jax.experimental.pallas import tpu as pltpu
from jax.sharding import PartitionSpec as P

NCLASS = 172
BLOCK = 64
STEPS = 3
CAP = 4
TELEPORT = 0.1
FILL = -1e30

HALF = 16
LANES = 128
PEER = CAP * HALF

F32 = jnp.float32
BF16 = jnp.bfloat16


def index_tables(block_slot, doms, row_blocks):
    entries = block_slot.shape[0]
    me = lax.axis_index("dom")
    chunks = (entries - (doms - 1) + row_blocks) // 2
    entry = jnp.arange(entries, dtype=jnp.int32)
    blocks = jnp.arange(row_blocks, dtype=jnp.int32)
    local = block_slot < row_blocks
    peer = (block_slot - row_blocks) // CAP
    place = (block_slot - row_blocks) % CAP
    came = jnp.where(local, block_slot, row_blocks + ((me - peer - 1) % doms) * CAP + place)
    goes = jnp.where(local, -1, ((peer - me - 1) % doms) * CAP + place)
    slots = jnp.arange(doms * CAP, dtype=jnp.int32)
    entry_of = jnp.sum(jnp.where(goes[None, :] == slots[:, None], entry[None, :], 0), axis=1)
    count = jnp.sum((block_slot[None, :] == blocks[:, None]).astype(jnp.int32), axis=1)
    pairs = (count + 1) // 2
    first = jnp.sum(jnp.where(blocks[None, :] < blocks[:, None], pairs[None, :], 0), axis=1)
    before = jnp.sum(jnp.where(blocks[None, :] < block_slot[:, None], pairs[None, :], 0), axis=1)
    same = (block_slot[None, :] == block_slot[:, None]) & (entry[None, :] < entry[:, None])
    rank = jnp.sum(same.astype(jnp.int32), axis=1)
    at = jnp.where(local, 2 * before + rank, -1)
    spots = jnp.arange(2 * chunks, dtype=jnp.int32)
    order = jnp.sum(jnp.where(at[None, :] == spots[:, None], entry[None, :] + 1, 0), axis=1) - 1
    chunk = jnp.arange(chunks, dtype=jnp.int32)
    starts = (first[None, :] == chunk[:, None]) & (count[None, :] > 0)
    keep = 1 - jnp.max(starts.astype(jnp.int32), axis=1)
    last = jnp.where(count > 0, first + pairs - 1, chunks)
    used = jnp.maximum(order, 0)
    lists = (
        came,
        entry_of // 2,
        entry_of % 2,
        entry_of // 8,
        used // 2,
        jnp.where(order < 0, 2, order % 2),
        used // 8,
        keep,
        last,
    )
    return jnp.concatenate([x.astype(jnp.int32) for x in lists]), chunks


def kernel(
    doms,
    cols,
    classes,
    chunks,
    index,
    features,
    w_hidden,
    w_out,
    tiles,
    request,
    code,
    prop_out,
    grad_out,
    head_send,
    stat_send,
    stat_recv,
    want,
    want_s,
    teleports,
    table0,
    table1,
    table2,
    swapped,
    inverse,
    final,
    grad,
    w_plain,
    w_swapped,
    acc,
    come_in,
    remote_tiles,
    local_tiles,
    route,
    out_buf,
    back_buf,
    head_sems,
    stat_sems,
    request_sems,
    local_sem,
    send_sems,
    recv_sems,
):
    me = lax.axis_index("dom")
    my_col = lax.axis_index("col")
    row_blocks = code.shape[0]
    entries = row_blocks * 8
    share = w_out.shape[1] // cols
    mine = features.shape[0] // BLOCK
    slots, spots = doms * CAP, 2 * chunks
    at_slot_tile = entries
    at_slot_half = at_slot_tile + slots
    at_slot_row = at_slot_half + slots
    at_tile = at_slot_row + slots
    at_half = at_tile + spots
    at_row = at_half + spots
    at_keep = at_row + spots
    at_last = at_keep + chunks
    peers = doms - 1
    local_rows = row_blocks * HALF
    table = (table0, table1, table2)

    lane = lax.broadcasted_iota(jnp.int32, (HALF, LANES), 1)
    low = lane < BLOCK

    def swap(x):
        return pltpu.roll(x, BLOCK, 1)

    def dom_at(shift):
        return lax.rem(me + shift, doms)

    def col_at(shift):
        return lax.rem(my_col + shift, cols)

    barrier = pltpu.get_barrier_semaphore()

    def greet_dom(k, carry):
        pl.semaphore_signal(barrier, inc=1, device_id={"dom": dom_at(k + 1)}, device_id_type=pl.DeviceIdType.MESH)
        return carry

    def greet_col(k, carry):
        pl.semaphore_signal(barrier, inc=1, device_id={"col": col_at(k + 1)}, device_id_type=pl.DeviceIdType.MESH)
        return carry

    lax.fori_loop(0, peers, greet_dom, 0)
    lax.fori_loop(0, cols - 1, greet_col, 0)

    hidden = jax.nn.relu(jnp.dot(features[...], w_hidden[...], preferred_element_type=F32)).astype(BF16)
    heads = jnp.dot(hidden, w_out[...], preferred_element_type=F32).T
    for c in range(cols):
        for pair in range(mine // 2):
            part = heads[c * share : (c + 1) * share, pair * LANES : (pair + 1) * LANES]
            top, bottom = part[:HALF], part[HALF:]
            at = c * mine + pair * 2
            head_send[at] = jnp.where(low, top, swap(bottom)).astype(BF16)
            head_send[at + 1] = jnp.where(low, swap(top), bottom).astype(BF16)

    pl.semaphore_wait(barrier, peers + cols - 1)

    def request_copy(k):
        return pltpu.make_async_remote_copy(
            src_ref=request.at[dom_at(k + 1)],
            dst_ref=want.at[k],
            send_sem=request_sems.at[0],
            recv_sem=request_sems.at[1],
            device_id={"dom": dom_at(k + 1)},
            device_id_type=pl.DeviceIdType.MESH,
        )

    def start_request(k, carry):
        request_copy(k).start()
        return carry

    lax.fori_loop(0, peers, start_request, 0)

    def own(col):
        return pl.ds(col * mine, mine)

    def head_copy(j):
        return pltpu.make_async_remote_copy(
            src_ref=head_send.at[own(col_at(j + 1))],
            dst_ref=teleports.at[own(my_col)],
            send_sem=head_sems.at[0, j],
            recv_sem=head_sems.at[1, j],
            device_id={"col": col_at(j + 1)},
            device_id_type=pl.DeviceIdType.MESH,
        )

    for j in range(cols - 1):
        head_copy(j).start()
    teleports[own(my_col)] = head_send[own(my_col)]

    def row_tiles(r):
        parts = [tiles[4 * r + q] for q in range(4)]
        return jnp.concatenate(parts, axis=1)

    ones = jnp.ones((HALF, 4 * LANES), BF16)
    contract_lanes = (((1,), (1,)), ((), ()))

    def degree(r, carry):
        sums = lax.dot_general(ones, row_tiles(r), contract_lanes, preferred_element_type=F32)
        inverse[r] = 1.0 / (1.0 + jnp.concatenate([sums, sums], axis=1))
        return carry

    lax.fori_loop(0, row_blocks, degree, 0, unroll=4)

    def all_requests(wait):
        whole = pltpu.make_async_remote_copy(
            src_ref=want.at[pl.ds(0, peers)],
            dst_ref=want.at[pl.ds(0, peers)],
            send_sem=request_sems.at[0],
            recv_sem=request_sems.at[1],
            device_id={"dom": dom_at(1)},
            device_id_type=pl.DeviceIdType.MESH,
        )
        whole.wait_recv() if wait == "recv" else whole.wait_send()

    all_requests("recv")
    want[peers] = jnp.full((1, LANES), row_blocks, jnp.int32)
    teleports[row_blocks] = jnp.zeros((HALF, LANES), BF16)
    w_plain[row_blocks] = jnp.zeros((HALF, LANES), BF16)
    to_scalars = pltpu.make_async_copy(want, want_s, local_sem.at[0])
    to_scalars.start()
    to_scalars.wait()

    for j in range(cols - 1):
        head_copy(j).wait_recv()

    def swap_first(r, carry):
        block = teleports[r]
        table0[r] = block
        swapped[0, r] = swap(block.astype(F32)).astype(BF16)
        return carry

    lax.fori_loop(0, row_blocks, swap_first, 0, unroll=4)

    def peer_copy(step, k):
        at = pl.ds(k * CAP, CAP)
        if step < STEPS:
            dst = table[step].at[pl.ds(row_blocks + k * CAP, CAP)]
        else:
            dst = back_buf.at[step - STEPS, at]
        return pltpu.make_async_remote_copy(
            src_ref=out_buf.at[step, at],
            dst_ref=dst,
            send_sem=send_sems.at[step],
            recv_sem=recv_sems.at[step],
            device_id={"dom": dom_at(k + 1)},
            device_id_type=pl.DeviceIdType.MESH,
        )

    def whole_copy(step):
        at = pl.ds(0, peers * CAP)
        dst = table[step].at[pl.ds(row_blocks, peers * CAP)] if step < STEPS else back_buf.at[step - STEPS, at]
        return pltpu.make_async_remote_copy(
            src_ref=out_buf.at[step, at],
            dst_ref=dst,
            send_sem=send_sems.at[step],
            recv_sem=recv_sems.at[step],
            device_id={"dom": dom_at(1)},
            device_id_type=pl.DeviceIdType.MESH,
        )

    def two_blocks(plain, turned, a, b):
        top = jnp.where(low, plain(a), turned(b))
        bottom = jnp.where(low, turned(a), plain(b))
        return jnp.concatenate([top, bottom], axis=0)

    side = jnp.where(lax.broadcasted_iota(jnp.int32, (BLOCK, LANES), 1) < BLOCK, 0, 1)

    def build_tiles(dst, n, start, half):
        pair = tiles[start].astype(F32)
        tile = jnp.where(side == half, pair, jnp.where(side == 1 - half, swap(pair), 0.0))
        dst[pl.ds(pl.multiple_of(n * BLOCK, BLOCK), BLOCK), :] = tile.astype(BF16)

    def build_remote(n, carry):
        build_tiles(remote_tiles, n, index[at_slot_tile + n], index[at_slot_half + n])
        return carry

    def build_local(n, carry):
        build_tiles(local_tiles, n, index[at_tile + n], index[at_half + n])
        return carry

    def build_route(m, carry):
        row = lax.broadcasted_iota(jnp.int32, (local_rows, LANES), 0)
        col = lax.broadcasted_iota(jnp.int32, (local_rows, LANES), 1)
        wide = lax.broadcasted_iota(jnp.int32, (1, LANES), 1) < BLOCK
        target = jnp.where(wide, want[2 * m], want[2 * m + 1])
        hit = row - col % HALF == target * HALF
        at = pl.ds(pl.multiple_of(m * local_rows, local_rows), local_rows)
        route[at, :] = jnp.where(hit, 1.0, 0.0).astype(BF16)
        return carry

    for step in range(STEPS):
        state_at = teleports if step == 0 else w_plain

        def send(k, carry):
            for c in range(CAP):
                block = want_s[peers - 1 - k, 0, HALF * c]
                out_buf[step, k * CAP + c] = state_at[block]
            peer_copy(step, k).start()
            return carry

        lax.fori_loop(0, peers, send, 0)
        if step == 0:
            lax.fori_loop(0, 2 * chunks, build_local, 0, unroll=2)
        elif step == 1:
            lax.fori_loop(0, peers * CAP, build_remote, 0, unroll=2)
        else:
            lax.fori_loop(0, doms // 2, build_route, 0)
            acc[chunks] = jnp.zeros((HALF, LANES), F32)
            for late in range(STEPS):
                back_buf[late, pl.ds(peers * CAP, CAP)] = jnp.zeros((CAP, HALF, LANES), BF16)
        whole_copy(step).wait_recv()

        def swap_remote(k, carry):
            at = row_blocks + k
            swapped[step, at] = swap(table[step][at].astype(F32)).astype(BF16)
            return carry

        lax.fori_loop(0, peers * CAP, swap_remote, 0, unroll=4)

        def plain(i):
            return table[step][i]

        def turned(i):
            return swapped[step, i]

        def propagate(r, carry):
            picked = [two_blocks(plain, turned, index[8 * r + 2 * q], index[8 * r + 2 * q + 1]) for q in range(4)]
            sums = lax.dot_general(
                jnp.concatenate(picked, axis=1), row_tiles(r), contract_lanes, preferred_element_type=F32
            )
            sums = jnp.concatenate([sums[:HALF], sums[HALF:]], axis=1)
            rounded = state_at[r].astype(F32)
            teleport = teleports[r].astype(F32)
            state = (1.0 - TELEPORT) * ((sums + rounded) * inverse[r]) + TELEPORT * teleport
            if step + 1 < STEPS:
                table[step + 1][r] = state.astype(BF16)
                w_plain[r] = state.astype(BF16)
                swapped[step + 1, r] = swap(state).astype(BF16)
            else:
                final[r] = state
            return carry

        lax.fori_loop(0, row_blocks, propagate, 0, unroll=4)

    low_row = lax.broadcasted_iota(jnp.int32, (1, LANES), 1) < BLOCK
    class_id = (
        my_col * share
        + lax.broadcasted_iota(jnp.int32, (HALF, LANES), 0)
        + jnp.where(low, 0, HALF)
    )
    usable = class_id < classes

    def statistics(r, carry):
        state = final[r]
        top = jnp.max(jnp.where(usable, state, FILL), axis=0, keepdims=True)
        top = jnp.maximum(top, swap(top))
        expo = jnp.where(usable, jnp.exp(state - top), 0.0)
        sums = jnp.sum(expo, axis=0, keepdims=True)
        sums = sums + swap(sums)
        stat_send[pl.ds(r, 1), :] = jnp.where(low_row, top, sums)
        return carry

    lax.fori_loop(0, row_blocks, statistics, 0, unroll=4)

    def stat_copy(j):
        return pltpu.make_async_remote_copy(
            src_ref=stat_send,
            dst_ref=stat_recv.at[j],
            send_sem=stat_sems.at[0, j],
            recv_sem=stat_sems.at[1, j],
            device_id={"col": col_at(j + 1)},
            device_id_type=pl.DeviceIdType.MESH,
        )

    for j in range(cols - 1):
        stat_copy(j).start()

    def unpack(source, dest):
        def pair(m, carry):
            first, second = source[2 * m], source[2 * m + 1]
            at = pl.ds(pl.multiple_of(m * LANES, LANES), LANES)
            dest[pl.ds(0, HALF), at] = jnp.where(low, first, swap(second))
            dest[pl.ds(HALF, HALF), at] = jnp.where(low, swap(first), second)
            return carry

        lax.fori_loop(0, row_blocks // 2, pair, 0, unroll=2)

    unpack(final, prop_out)
    for j in range(cols - 1):
        stat_copy(j).wait_recv()

    wide_low = lax.broadcasted_iota(jnp.int32, (row_blocks, LANES), 1) < BLOCK
    stats = [stat_send[...]] + [stat_recv[j] for j in range(cols - 1)]
    tops = [jnp.where(wide_low, s, swap(s)) for s in stats]
    sums = [jnp.where(wide_low, swap(s), s) for s in stats]
    top = functools.reduce(jnp.maximum, tops)
    whole = functools.reduce(jnp.add, [s * jnp.exp(t - top) for s, t in zip(sums, tops)])
    stat_send_free = [stat_copy(j) for j in range(cols - 1)]
    for copy in stat_send_free:
        copy.wait_send()
    stat_send[...] = top
    stat_recv[0] = 1.0 / whole

    def store_scaled(r, gradient):
        scaled = inverse[r] * gradient
        w_plain[r] = scaled.astype(BF16)
        w_swapped[r] = swap(scaled).astype(BF16)

    def cotangent(r, carry):
        state = final[r]
        expo = jnp.exp(state - stat_send[pl.ds(r, 1), :])
        probs = expo * stat_recv[0, pl.ds(r, 1), :]
        coded = code[r]
        onehot = jnp.where(class_id == coded % 256, 1.0, 0.0)
        weight = (coded // 256).astype(F32)
        gradient = jnp.where(usable, weight * (probs - onehot), 0.0)
        grad[r] = TELEPORT * gradient
        store_scaled(r, gradient)
        return carry

    lax.fori_loop(0, row_blocks, cotangent, 0, unroll=2)

    nothing = jnp.zeros((HALF, LANES), BF16)

    def w_at(i):
        return w_plain[i]

    def w_turned(i):
        return w_swapped[i]

    for late in range(STEPS):

        def send_back(k, carry):
            lines = []
            for c in range(CAP):
                r = index[at_slot_row + CAP * k + c]
                if c % 2 == 0:
                    top, bottom = jnp.where(low, w_at(r), nothing), jnp.where(low, w_turned(r), nothing)
                else:
                    top, bottom = jnp.where(low, nothing, w_turned(r)), jnp.where(low, nothing, w_at(r))
                here = jnp.concatenate([top, bottom], axis=0)
                blank = jnp.zeros_like(here)
                lines.append(jnp.concatenate([here, blank] if c < 2 else [blank, here], axis=1))
            weights = remote_tiles[pl.ds(pl.multiple_of(k * CAP * BLOCK, CAP * BLOCK), CAP * BLOCK), :]
            products = jnp.dot(jnp.concatenate(lines, axis=0), weights, preferred_element_type=F32)
            for c in range(CAP):
                top = products[2 * c * HALF : (2 * c + 1) * HALF]
                bottom = products[(2 * c + 1) * HALF : (2 * c + 2) * HALF]
                out_buf[STEPS + late, k * CAP + c] = jnp.where(low, top, bottom).astype(BF16)
            peer_copy(STEPS + late, k).start()
            return carry

        lax.fori_loop(0, peers, send_back, 0)

        def local_chunk(m, running):
            a, b = index[at_row + 2 * m], index[at_row + 2 * m + 1]
            weights = local_tiles[pl.ds(pl.multiple_of(m * 2 * BLOCK, 2 * BLOCK), 2 * BLOCK), :]
            products = jnp.dot(two_blocks(w_at, w_turned, a, b), weights, preferred_element_type=F32)
            term = jnp.where(low, products[:HALF], products[HALF:])
            running = running * index[at_keep + m].astype(F32) + term
            acc[m] = running
            return running

        lax.fori_loop(0, chunks, local_chunk, jnp.zeros((HALF, LANES), F32), unroll=4)

        def local_sum(r, carry):
            come_in[r] = acc[index[at_last + r]]
            return carry

        lax.fori_loop(0, row_blocks, local_sum, 0, unroll=4)
        whole_copy(STEPS + late).wait_recv()

        def arrive(m, carry):
            left = route[pl.ds(pl.multiple_of(2 * m * local_rows, local_rows), local_rows), :]
            right = route[pl.ds(pl.multiple_of((2 * m + 1) * local_rows, local_rows), local_rows), :]
            part = back_buf[late, pl.ds(m * 4 * CAP, 4 * CAP)].reshape(4 * PEER, LANES)
            sums = jnp.dot(jnp.concatenate([left, right], axis=1), part, preferred_element_type=F32)
            come_in[...] += sums.reshape(row_blocks, HALF, LANES)
            return carry

        lax.fori_loop(0, doms // 4, arrive, 0)

        def finish(r, carry):
            gradient = (1.0 - TELEPORT) * (come_in[r] + w_plain[r].astype(F32))
            if late < STEPS - 1:
                grad[r] += TELEPORT * gradient
                store_scaled(r, gradient)
            else:
                grad[r] += gradient
            return carry

        lax.fori_loop(0, row_blocks, finish, 0, unroll=4)

    unpack(grad, grad_out)

    all_requests("send")
    for j in range(cols - 1):
        head_copy(j).wait_send()
    for step in range(2 * STEPS):
        whole_copy(step).wait_send()


def body(features, w_hidden, w_out, block_values, block_slot, requested, labels, train_mask):
    doms, cols = lax.axis_size("dom"), lax.axis_size("col")
    nodes = labels.shape[0]
    row_blocks = nodes // BLOCK
    share = w_out.shape[1] // cols
    entries = block_slot.shape[0]
    index, chunks = index_tables(block_slot, doms, row_blocks)
    tiles = (
        block_values.reshape(entries // 2, 2, BLOCK, BLOCK).transpose(0, 2, 1, 3).reshape(entries // 2, BLOCK, LANES)
    )
    asked = jnp.where(requested < 0, row_blocks, requested)
    request = jnp.broadcast_to(asked.reshape(doms, 1, 1, CAP, 1), (doms, 1, 2, CAP, HALF)).reshape(doms, 1, LANES)
    code = (labels + 256 * train_mask).reshape(row_blocks, 1, 1, BLOCK)
    code = jnp.broadcast_to(code, (row_blocks, 1, 2, BLOCK)).reshape(row_blocks, 1, LANES)
    peers = doms - 1
    local_rows = row_blocks * HALF
    all_blocks = row_blocks + doms * CAP
    vmem, dma = pltpu.VMEM, pltpu.SemaphoreType.DMA
    mine = features.shape[0] // BLOCK
    in_vmem = pl.BlockSpec(memory_space=pltpu.VMEM)
    return pl.pallas_call(
        functools.partial(kernel, doms, cols, NCLASS, chunks),
        out_shape=[jax.ShapeDtypeStruct((share, nodes), F32)] * 2,
        in_specs=[pl.BlockSpec(memory_space=pltpu.SMEM)] + [in_vmem] * 6,
        out_specs=[in_vmem] * 2,
        scratch_shapes=[
            vmem((cols * mine, HALF, LANES), BF16),
            vmem((row_blocks, LANES), F32),
            vmem((cols - 1, row_blocks, LANES), F32),
            vmem((doms, 1, LANES), jnp.int32),
            pltpu.SMEM((doms, 1, LANES), jnp.int32),
            vmem((row_blocks + 1, HALF, LANES), BF16),
            vmem((all_blocks, HALF, LANES), BF16),
            vmem((all_blocks, HALF, LANES), BF16),
            vmem((all_blocks, HALF, LANES), BF16),
            vmem((STEPS, all_blocks, HALF, LANES), BF16),
            vmem((row_blocks, HALF, LANES), F32),
            vmem((row_blocks, HALF, LANES), F32),
            vmem((row_blocks, HALF, LANES), F32),
            vmem((row_blocks + 1, HALF, LANES), BF16),
            vmem((row_blocks, HALF, LANES), BF16),
            vmem((chunks + 1, HALF, LANES), F32),
            vmem((row_blocks, HALF, LANES), F32),
            vmem((peers * CAP * BLOCK, LANES), BF16),
            vmem((2 * chunks * BLOCK, LANES), BF16),
            vmem((doms // 2 * local_rows, LANES), BF16),
            vmem((2 * STEPS, peers * CAP, HALF, LANES), BF16),
            vmem((STEPS, doms * CAP, HALF, LANES), BF16),
            dma((2, cols - 1)),
            dma((2, cols - 1)),
            dma((2,)),
            dma((1,)),
            dma((2 * STEPS,)),
            dma((2 * STEPS,)),
        ],
        compiler_params=pltpu.CompilerParams(
            collective_id=0, has_side_effects=True, vmem_limit_bytes=48 * 2**20
        ),
    )(index, features, w_hidden, w_out, tiles, request, code)


def solution(mesh):
    return jax.shard_map(
        body,
        mesh=mesh,
        in_specs=(
            P(("dom", "col"), None),
            P(),
            P(),
            P("dom", None),
            P("dom"),
            P("dom", None, None),
            P("dom"),
            P("dom"),
        ),
        out_specs=(P("col", "dom"), P("col", "dom")),
        check_vma=False,
    )
```

profile of v0, /device:TPU:1, one launch (start us, length us, event | category | flops | bytes accessed | tf_op | source)
XLA Modules:
  0.0 172.1 jit_solution(5020303121076989990)
XLA Ops:
  0.6 0.8 convert_reduce_fusion.1
  1.4 0.8 select_reduce_fusion.2
  2.2 0.9 convert_reduce_fusion
  3.1 0.7 add_select_fusion
  3.9 0.1 select_reduce_fusion.1
  4.0 0.1 select_reduce_fusion
  4.2 0.1 select_reduce_fusion.3
  4.3 0.1 convert_reduce_fusion.2
  4.4 6.9 %reshape.58 = bf16[128,2,64,64]{3,2,1,0:T(8,128)(2,1)} reshape(bf16[256,4096]{1,0:T(8,128)(2,1)} %param.11) | data formatting | bytes 4194304 | tf_op jit(solution)/shard_map/reshape | solution.py:519
  11.3 6.5 %copy.15 = bf16[128,64,2,64]{0,3,2,1:T(8,128)(2,1)} copy(bf16[128,64,2,64]{3,1,2,0:T(8,128)(2,1)} %bitcast.5) | data formatting | bytes 4194304 | tf_op jit(solution)/shard_map/transpose | solution.py:519
  17.8 0.0 copy-start.5
  17.8 0.0 copy-start.3
  17.8 0.0 copy-start.4
  17.8 0.0 copy-start
  17.8 0.0 copy-start.1
  17.8 0.0 copy-start.2
  17.8 3.4 %copy.16.tiles = bf16[128,64,128]{2,1,0:T(8,128)(2,1)S(1)} copy(bf16[128,64,128]{0,2,1:T(8,128)(2,1)} %bitcast.6) | data formatting | bytes 4194304 | tf_op jit(solution)/shard_map/reshape | solution.py:519
  21.2 0.0 copy-done.5
  21.3 0.1 copy.17.request
  21.3 0.0 copy-done.3
  21.3 0.0 copy-done.4
  21.4 0.1 broadcast_in_dim.113
  21.5 0.1 broadcast_in_dim.115.code
  21.6 0.0 copy-done
  21.6 0.0 copy-done.1
  21.6 0.0 copy-done.2
  21.6 149.1 %shard_map.95 = (f32[32,2048]{1,0:T(8,128)S(1)}, f32[32,2048]{1,0:T(8,128)S(1)}) custom-call(s32[1568]{0:T(1024)S(1)} %constant_dynamic-update-slice_fusion.index, bf16[256,128]{1,0:T(8,128)(2,1)S(1)} %copy-done.1, bf16[128,256]{1,0:T(8,128)(2,1)S(1)} %copy-done.2, bf16[256,256]{1,0:T(8,128)(2,1)S(1)} %copy-done, bf16[128,64,128]{2,1,0:T(8,128)(2,1)S(1)} %copy.16.tiles, ...), custom_call_target="tpu_custom_call" | custom-call | tf_op jit(solution)/shard_map/pallas_call | solution.py:531
  170.7 0.7 copy.29
  171.4 0.7 copy.30
  (15 shorter events, 0.2 us)
Async XLA Ops:
  17.8 3.4 %copy-start.5 = (s32[1,32,4]{1,2,0:T(4,128)S(1)}, s32[1,32,4]{1,2,0:T(4,128)}, u32[]{:S(2)}) copy-start(s32[1,32,4]{1,2,0:T(4,128)} %param.13) | copy-start | bytes 1540
  17.8 3.5 %copy-start.3 = (s32[2048]{0:T(1024)S(1)}, s32[2048]{0:T(1024)}, u32[]{:S(2)}) copy-start(s32[2048]{0:T(1024)} %param.14) | copy-start | bytes 24580
  17.8 3.5 %copy-start.4 = (s32[2048]{0:T(1024)S(1)}, s32[2048]{0:T(1024)}, u32[]{:S(2)}) copy-start(s32[2048]{0:T(1024)} %param.15) | copy-start | bytes 24580
  17.8 3.8 %copy-start = (bf16[256,256]{1,0:T(8,128)(2,1)S(1)}, bf16[256,256]{1,0:T(8,128)(2,1)}, u32[]{:S(2)}) copy-start(bf16[256,256]{1,0:T(8,128)(2,1)} %w_out.1) | copy-start | bytes 393220
  17.8 3.8 %copy-start.1 = (bf16[256,128]{1,0:T(8,128)(2,1)S(1)}, bf16[256,128]{1,0:T(8,128)(2,1)}, u32[]{:S(2)}) copy-start(bf16[256,128]{1,0:T(8,128)(2,1)} %features.1) | copy-start | bytes 196612
  17.8 3.8 %copy-start.2 = (bf16[128,256]{1,0:T(8,128)(2,1)S(1)}, bf16[128,256]{1,0:T(8,128)(2,1)}, u32[]{:S(2)}) copy-start(bf16[128,256]{1,0:T(8,128)(2,1)} %w_hidden.1) | copy-start | bytes 196612
where the time goes:
time: 173 us; the launch traced here: 172 us
  Pallas kernels  149 us (86%)
  local copies, waits for them, and re-layouts  18.4 us (11%)
  other arithmetic  3.76 us (2%)
    pallas_call x1, Pallas kernels, body(): pl.pallas_call(functools.partial(kernel, doms, cols, NCLASS, chunks), out...  149 us
    reshape x2, local copies, waits for them, and re-layouts, body(): block_values.reshape(entries // 2, 2, BLOCK, BLOCK).transpose(0, 2, 1, 3)  10.3 us
    transpose x1, local copies, waits for them, and re-layouts, body(): block_values.reshape(entries // 2, 2, BLOCK, BLOCK).transpose(0, 2, 1, 3)  6.47 us

commit v1 on v0

--- a/solution.py
+++ b/solution.py
@@ -17,6 +17,7 @@
 HALF = 16
 LANES = 128
 PEER = CAP * HALF
+GROUP = 8
 
 F32 = jnp.float32
 BF16 = jnp.bfloat16
@@ -25,7 +26,7 @@
 def index_tables(block_slot, doms, row_blocks):
     entries = block_slot.shape[0]
     me = lax.axis_index("dom")
-    chunks = (entries - (doms - 1) + row_blocks) // 2
+    chunks = -(-((entries - (doms - 1) + row_blocks) // 2) // GROUP) * GROUP
     entry = jnp.arange(entries, dtype=jnp.int32)
     blocks = jnp.arange(row_blocks, dtype=jnp.int32)
     local = block_slot < row_blocks
@@ -86,7 +87,9 @@
     table0,
     table1,
     table2,
-    swapped,
+    swapped0,
+    swapped1,
+    swapped2,
     inverse,
     final,
     grad,
@@ -124,6 +127,7 @@
     peers = doms - 1
     local_rows = row_blocks * HALF
     table = (table0, table1, table2)
+    swapped = (swapped0, swapped1, swapped2)
 
     lane = lax.broadcasted_iota(jnp.int32, (HALF, LANES), 1)
     low = lane < BLOCK
@@ -231,13 +235,19 @@
     for j in range(cols - 1):
         head_copy(j).wait_recv()
 
-    def swap_first(r, carry):
-        block = teleports[r]
-        table0[r] = block
-        swapped[0, r] = swap(block.astype(F32)).astype(BF16)
-        return carry
-
-    lax.fori_loop(0, row_blocks, swap_first, 0, unroll=4)
+    def turn(blocks):
+        count = blocks.shape[0]
+        flat = swap(blocks.astype(F32).reshape(count * HALF, LANES))
+        return flat.astype(BF16).reshape(count, HALF, LANES)
+
+    def swap_first(group, carry):
+        at = pl.ds(group * GROUP, GROUP)
+        blocks = teleports[at]
+        table0[at] = blocks
+        swapped[0][at] = turn(blocks)
+        return carry
+
+    lax.fori_loop(0, row_blocks // GROUP, swap_first, 0)
 
     def peer_copy(step, k):
         at = pl.ds(k * CAP, CAP)
@@ -273,17 +283,22 @@
 
     side = jnp.where(lax.broadcasted_iota(jnp.int32, (BLOCK, LANES), 1) < BLOCK, 0, 1)
 
-    def build_tiles(dst, n, start, half):
+    def built(start, half):
         pair = tiles[start].astype(F32)
-        tile = jnp.where(side == half, pair, jnp.where(side == 1 - half, swap(pair), 0.0))
-        dst[pl.ds(pl.multiple_of(n * BLOCK, BLOCK), BLOCK), :] = tile.astype(BF16)
-
-    def build_remote(n, carry):
-        build_tiles(remote_tiles, n, index[at_slot_tile + n], index[at_slot_half + n])
-        return carry
-
-    def build_local(n, carry):
-        build_tiles(local_tiles, n, index[at_tile + n], index[at_half + n])
+        return jnp.where(side == half, pair, jnp.where(side == 1 - half, swap(pair), 0.0)).astype(BF16)
+
+    def build_tiles(dst, group, at_start, at_side):
+        first = group * 4
+        made = [built(index[at_start + first + i], index[at_side + first + i]) for i in range(4)]
+        at = pl.ds(pl.multiple_of(first * BLOCK, 4 * BLOCK), 4 * BLOCK)
+        dst[at, :] = jnp.concatenate(made, axis=0)
+
+    def build_remote(group, carry):
+        build_tiles(remote_tiles, group, at_slot_tile, at_slot_half)
+        return carry
+
+    def build_local(group, carry):
+        build_tiles(local_tiles, group, at_tile, at_half)
         return carry
 
     def build_route(m, carry):
@@ -308,9 +323,9 @@
 
         lax.fori_loop(0, peers, send, 0)
         if step == 0:
-            lax.fori_loop(0, 2 * chunks, build_local, 0, unroll=2)
+            lax.fori_loop(0, chunks // 2, build_local, 0)
         elif step == 1:
-            lax.fori_loop(0, peers * CAP, build_remote, 0, unroll=2)
+            lax.fori_loop(0, peers, build_remote, 0)
         else:
             lax.fori_loop(0, doms // 2, build_route, 0)
             acc[chunks] = jnp.zeros((HALF, LANES), F32)
@@ -318,39 +333,50 @@
                 back_buf[late, pl.ds(peers * CAP, CAP)] = jnp.zeros((CAP, HALF, LANES), BF16)
         whole_copy(step).wait_recv()
 
-        def swap_remote(k, carry):
-            at = row_blocks + k
-            swapped[step, at] = swap(table[step][at].astype(F32)).astype(BF16)
-            return carry
-
-        lax.fori_loop(0, peers * CAP, swap_remote, 0, unroll=4)
+        def swap_remote(at):
+            swapped[step][at] = turn(table[step][at])
+
+        def swap_group(group, carry):
+            swap_remote(pl.ds(row_blocks + group * 2 * GROUP, 2 * GROUP))
+            return carry
+
+        whole_groups = peers * CAP // (2 * GROUP)
+        lax.fori_loop(0, whole_groups, swap_group, 0)
+        swap_remote(pl.ds(row_blocks + whole_groups * 2 * GROUP, peers * CAP - whole_groups * 2 * GROUP))
 
         def plain(i):
             return table[step][i]
 
         def turned(i):
-            return swapped[step, i]
-
-        def propagate(r, carry):
-            picked = [two_blocks(plain, turned, index[8 * r + 2 * q], index[8 * r + 2 * q + 1]) for q in range(4)]
-            sums = lax.dot_general(
-                jnp.concatenate(picked, axis=1), row_tiles(r), contract_lanes, preferred_element_type=F32
-            )
-            sums = jnp.concatenate([sums[:HALF], sums[HALF:]], axis=1)
-            rounded = state_at[r].astype(F32)
-            teleport = teleports[r].astype(F32)
-            state = (1.0 - TELEPORT) * ((sums + rounded) * inverse[r]) + TELEPORT * teleport
+            return swapped[step][i]
+
+        def propagate(group, carry):
+            rows = [group * GROUP + i for i in range(GROUP)]
+            sums = []
+            for r in rows:
+                picked = [two_blocks(plain, turned, index[8 * r + 2 * q], index[8 * r + 2 * q + 1]) for q in range(4)]
+                sums.append(
+                    lax.dot_general(
+                        jnp.concatenate(picked, axis=1), row_tiles(r), contract_lanes, preferred_element_type=F32
+                    )
+                )
+            sums = jnp.stack([jnp.concatenate([x[:HALF], x[HALF:]], axis=1) for x in sums])
+            at = pl.ds(group * GROUP, GROUP)
+            rounded, teleport = state_at[at].astype(F32), teleports[at].astype(F32)
+            state = (1.0 - TELEPORT) * ((sums + rounded) * inverse[at]) + TELEPORT * teleport
             if step + 1 < STEPS:
-                table[step + 1][r] = state.astype(BF16)
-                w_plain[r] = state.astype(BF16)
-                swapped[step + 1, r] = swap(state).astype(BF16)
+                blocks = state.astype(BF16)
+                flipped = turn(blocks)
+                table[step + 1][at] = blocks
+                w_plain[at] = blocks
+                swapped[step + 1][at] = flipped
             else:
-                final[r] = state
-            return carry
-
-        lax.fori_loop(0, row_blocks, propagate, 0, unroll=4)
-
-    low_row = lax.broadcasted_iota(jnp.int32, (1, LANES), 1) < BLOCK
+                final[at] = state
+            return carry
+
+        lax.fori_loop(0, row_blocks // GROUP, propagate, 0)
+
+    low_group = lax.broadcasted_iota(jnp.int32, (GROUP, LANES), 1) < BLOCK
     class_id = (
         my_col * share
         + lax.broadcasted_iota(jnp.int32, (HALF, LANES), 0)
@@ -358,17 +384,18 @@
     )
     usable = class_id < classes
 
-    def statistics(r, carry):
-        state = final[r]
-        top = jnp.max(jnp.where(usable, state, FILL), axis=0, keepdims=True)
+    def statistics(group, carry):
+        at = pl.ds(pl.multiple_of(group * GROUP, GROUP), GROUP)
+        state = final[at]
+        top = jnp.max(jnp.where(usable, state, FILL), axis=1)
         top = jnp.maximum(top, swap(top))
-        expo = jnp.where(usable, jnp.exp(state - top), 0.0)
-        sums = jnp.sum(expo, axis=0, keepdims=True)
+        expo = jnp.where(usable, jnp.exp(state - top[:, None, :]), 0.0)
+        sums = jnp.sum(expo, axis=1)
         sums = sums + swap(sums)
-        stat_send[pl.ds(r, 1), :] = jnp.where(low_row, top, sums)
-        return carry
-
-    lax.fori_loop(0, row_blocks, statistics, 0, unroll=4)
+        stat_send[at, :] = jnp.where(low_group, top, sums)
+        return carry
+
+    lax.fori_loop(0, row_blocks // GROUP, statistics, 0)
 
     def stat_copy(j):
         return pltpu.make_async_remote_copy(
@@ -409,24 +436,25 @@
     stat_send[...] = top
     stat_recv[0] = 1.0 / whole
 
-    def store_scaled(r, gradient):
-        scaled = inverse[r] * gradient
-        w_plain[r] = scaled.astype(BF16)
-        w_swapped[r] = swap(scaled).astype(BF16)
-
-    def cotangent(r, carry):
-        state = final[r]
-        expo = jnp.exp(state - stat_send[pl.ds(r, 1), :])
-        probs = expo * stat_recv[0, pl.ds(r, 1), :]
-        coded = code[r]
+    def store_scaled(at, gradient):
+        scaled = (inverse[at] * gradient).astype(BF16)
+        flipped = turn(scaled)
+        w_plain[at] = scaled
+        w_swapped[at] = flipped
+
+    def cotangent(group, carry):
+        at = pl.ds(pl.multiple_of(group * GROUP, GROUP), GROUP)
+        expo = jnp.exp(final[at] - stat_send[at, :][:, None, :])
+        probs = expo * stat_recv[0, at, :][:, None, :]
+        coded = code[at]
         onehot = jnp.where(class_id == coded % 256, 1.0, 0.0)
         weight = (coded // 256).astype(F32)
         gradient = jnp.where(usable, weight * (probs - onehot), 0.0)
-        grad[r] = TELEPORT * gradient
-        store_scaled(r, gradient)
-        return carry
-
-    lax.fori_loop(0, row_blocks, cotangent, 0, unroll=2)
+        grad[at] = TELEPORT * gradient
+        store_scaled(at, gradient)
+        return carry
+
+    lax.fori_loop(0, row_blocks // GROUP, cotangent, 0)
 
     nothing = jnp.zeros((HALF, LANES), BF16)
 
@@ -438,7 +466,7 @@
 
     for late in range(STEPS):
 
-        def send_back(k, carry):
+        def products_for(k):
             lines = []
             for c in range(CAP):
                 r = index[at_slot_row + CAP * k + c]
@@ -451,31 +479,46 @@
                 lines.append(jnp.concatenate([here, blank] if c < 2 else [blank, here], axis=1))
             weights = remote_tiles[pl.ds(pl.multiple_of(k * CAP * BLOCK, CAP * BLOCK), CAP * BLOCK), :]
             products = jnp.dot(jnp.concatenate(lines, axis=0), weights, preferred_element_type=F32)
-            for c in range(CAP):
-                top = products[2 * c * HALF : (2 * c + 1) * HALF]
-                bottom = products[(2 * c + 1) * HALF : (2 * c + 2) * HALF]
-                out_buf[STEPS + late, k * CAP + c] = jnp.where(low, top, bottom).astype(BF16)
-            peer_copy(STEPS + late, k).start()
-            return carry
-
-        lax.fori_loop(0, peers, send_back, 0)
-
-        def local_chunk(m, running):
-            a, b = index[at_row + 2 * m], index[at_row + 2 * m + 1]
-            weights = local_tiles[pl.ds(pl.multiple_of(m * 2 * BLOCK, 2 * BLOCK), 2 * BLOCK), :]
-            products = jnp.dot(two_blocks(w_at, w_turned, a, b), weights, preferred_element_type=F32)
-            term = jnp.where(low, products[:HALF], products[HALF:])
-            running = running * index[at_keep + m].astype(F32) + term
-            acc[m] = running
+            products = products.reshape(CAP, 2, HALF, LANES)
+            return jnp.where(low, products[:, 0], products[:, 1]).astype(BF16)
+
+        def send_back(first, count):
+            ready = [products_for(first + i) for i in range(count)]
+            for i, blocks in enumerate(ready):
+                out_buf[STEPS + late, pl.ds((first + i) * CAP, CAP)] = blocks
+            for i in range(count):
+                peer_copy(STEPS + late, first + i).start()
+
+        def send_group(group, carry):
+            send_back(group * 4, 4)
+            return carry
+
+        lax.fori_loop(0, peers // 4, send_group, 0)
+        send_back(peers // 4 * 4, peers % 4)
+
+        def local_chunks(group, running):
+            terms = []
+            for i in range(GROUP):
+                m = group * GROUP + i
+                a, b = index[at_row + 2 * m], index[at_row + 2 * m + 1]
+                weights = local_tiles[pl.ds(pl.multiple_of(m * 2 * BLOCK, 2 * BLOCK), 2 * BLOCK), :]
+                products = jnp.dot(two_blocks(w_at, w_turned, a, b), weights, preferred_element_type=F32)
+                terms.append(jnp.where(low, products[:HALF], products[HALF:]))
+            sums = []
+            for i in range(GROUP):
+                running = running * index[at_keep + group * GROUP + i].astype(F32) + terms[i]
+                sums.append(running)
+            acc[pl.ds(group * GROUP, GROUP)] = jnp.stack(sums)
             return running
 
-        lax.fori_loop(0, chunks, local_chunk, jnp.zeros((HALF, LANES), F32), unroll=4)
-
-        def local_sum(r, carry):
-            come_in[r] = acc[index[at_last + r]]
-            return carry
-
-        lax.fori_loop(0, row_blocks, local_sum, 0, unroll=4)
+        lax.fori_loop(0, chunks // GROUP, local_chunks, jnp.zeros((HALF, LANES), F32))
+
+        def local_sum(group, carry):
+            picked = [acc[index[at_last + group * GROUP + i]] for i in range(GROUP)]
+            come_in[pl.ds(group * GROUP, GROUP)] = jnp.stack(picked)
+            return carry
+
+        lax.fori_loop(0, row_blocks // GROUP, local_sum, 0)
         whole_copy(STEPS + late).wait_recv()
 
         def arrive(m, carry):
@@ -488,16 +531,17 @@
 
         lax.fori_loop(0, doms // 4, arrive, 0)
 
-        def finish(r, carry):
-            gradient = (1.0 - TELEPORT) * (come_in[r] + w_plain[r].astype(F32))
+        def finish(group, carry):
+            at = pl.ds(group * GROUP, GROUP)
+            gradient = (1.0 - TELEPORT) * (come_in[at] + w_plain[at].astype(F32))
             if late < STEPS - 1:
-                grad[r] += TELEPORT * gradient
-                store_scaled(r, gradient)
+                grad[at] += TELEPORT * gradient
+                store_scaled(at, gradient)
             else:
-                grad[r] += gradient
-            return carry
-
-        lax.fori_loop(0, row_blocks, finish, 0, unroll=4)
+                grad[at] += gradient
+            return carry
+
+        lax.fori_loop(0, row_blocks // GROUP, finish, 0)
 
     unpack(grad, grad_out)
 
@@ -543,7 +587,9 @@
             vmem((all_blocks, HALF, LANES), BF16),
             vmem((all_blocks, HALF, LANES), BF16),
             vmem((all_blocks, HALF, LANES), BF16),
-            vmem((STEPS, all_blocks, HALF, LANES), BF16),
+            vmem((all_blocks, HALF, LANES), BF16),
+            vmem((all_blocks, HALF, LANES), BF16),
+            vmem((all_blocks, HALF, LANES), BF16),
             vmem((row_blocks, HALF, LANES), F32),
             vmem((row_blocks, HALF, LANES), F32),
             vmem((row_blocks, HALF, LANES), F32),

time: 173 us -> 147 us (0.85)
  Pallas kernels: 149 us -> 124 us
    pallas_call x1, Pallas kernels: 149 us -> 124 us  [body(): pl.pallas_call(functools.partial(kernel, doms, cols, NCLASS, chunks), out...]
where the time goes in v1:
time: 147 us
  Pallas kernels  124 us (84%)
  local copies, waits for them, and re-layouts  18.4 us (13%)
  other arithmetic  3.76 us (3%)
    pallas_call x1, Pallas kernels, body(): pl.pallas_call(functools.partial(kernel, doms, cols, NCLASS, chunks), out...  124 us
    reshape x2, local copies, waits for them, and re-layouts, body(): block_values.reshape(entries // 2, 2, BLOCK, BLOCK).transpose(0, 2, 1, 3)  10.3 us
    transpose x1, local copies, waits for them, and re-layouts, body(): block_values.reshape(entries // 2, 2, BLOCK, BLOCK).transpose(0, 2, 1, 3)  6.47 us

profile of v1, /device:TPU:1, one launch (start us, length us, event | category | flops | bytes accessed | tf_op | source)
XLA Modules:
  0.0 146.8 jit_solution(3339285655563308586)
XLA Ops:
  0.6 0.8 convert_reduce_fusion.1
  1.4 0.8 select_reduce_fusion.2
  2.2 0.9 convert_reduce_fusion
  3.1 0.7 add_select_fusion
  3.9 0.1 select_reduce_fusion.1
  4.0 0.1 select_reduce_fusion
  4.2 0.1 select_reduce_fusion.3
  4.3 0.1 convert_reduce_fusion.2
  4.4 6.9 %reshape.58 = bf16[128,2,64,64]{3,2,1,0:T(8,128)(2,1)} reshape(bf16[256,4096]{1,0:T(8,128)(2,1)} %param.11) | data formatting | bytes 4194304 | tf_op jit(solution)/shard_map/reshape | solution.py:563
  11.3 6.5 %copy.15 = bf16[128,64,2,64]{0,3,2,1:T(8,128)(2,1)} copy(bf16[128,64,2,64]{3,1,2,0:T(8,128)(2,1)} %bitcast.5) | data formatting | bytes 4194304 | tf_op jit(solution)/shard_map/transpose | solution.py:563
  17.8 0.0 copy-start.5
  17.8 0.0 copy-start.3
  17.8 0.0 copy-start.4
  17.8 0.0 copy-start
  17.8 0.0 copy-start.1
  17.8 0.0 copy-start.2
  17.8 3.4 %copy.16.tiles = bf16[128,64,128]{2,1,0:T(8,128)(2,1)S(1)} copy(bf16[128,64,128]{0,2,1:T(8,128)(2,1)} %bitcast.6) | data formatting | bytes 4194304 | tf_op jit(solution)/shard_map/reshape | solution.py:563
  21.2 0.0 copy-done.5
  21.3 0.1 copy.17.request
  21.3 0.0 copy-done.3
  21.3 0.0 copy-done.4
  21.4 0.1 broadcast_in_dim.113
  21.5 0.1 broadcast_in_dim.115.code
  21.6 0.0 copy-done
  21.6 0.0 copy-done.1
  21.6 0.0 copy-done.2
  21.6 123.8 %shard_map.95 = (f32[32,2048]{1,0:T(8,128)S(1)}, f32[32,2048]{1,0:T(8,128)S(1)}) custom-call(s32[1568]{0:T(1024)S(1)} %constant_dynamic-update-slice_fusion.index, bf16[256,128]{1,0:T(8,128)(2,1)S(1)} %copy-done.1, bf16[128,256]{1,0:T(8,128)(2,1)S(1)} %copy-done.2, bf16[256,256]{1,0:T(8,128)(2,1)S(1)} %copy-done, bf16[128,64,128]{2,1,0:T(8,128)(2,1)S(1)} %copy.16.tiles, ...), custom_call_target="tpu_custom_call" | custom-call | tf_op jit(solution)/shard_map/pallas_call | solution.py:575
  145.4 0.7 copy.29
  146.1 0.7 copy.30
  (15 shorter events, 0.2 us)
Async XLA Ops:
  17.8 3.4 %copy-start.5 = (s32[1,32,4]{1,2,0:T(4,128)S(1)}, s32[1,32,4]{1,2,0:T(4,128)}, u32[]{:S(2)}) copy-start(s32[1,32,4]{1,2,0:T(4,128)} %param.13) | copy-start | bytes 1540
  17.8 3.5 %copy-start.3 = (s32[2048]{0:T(1024)S(1)}, s32[2048]{0:T(1024)}, u32[]{:S(2)}) copy-start(s32[2048]{0:T(1024)} %param.14) | copy-start | bytes 24580
  17.8 3.5 %copy-start.4 = (s32[2048]{0:T(1024)S(1)}, s32[2048]{0:T(1024)}, u32[]{:S(2)}) copy-start(s32[2048]{0:T(1024)} %param.15) | copy-start | bytes 24580
  17.8 3.8 %copy-start = (bf16[256,256]{1,0:T(8,128)(2,1)S(1)}, bf16[256,256]{1,0:T(8,128)(2,1)}, u32[]{:S(2)}) copy-start(bf16[256,256]{1,0:T(8,128)(2,1)} %w_out.1) | copy-start | bytes 393220
  17.8 3.8 %copy-start.1 = (bf16[256,128]{1,0:T(8,128)(2,1)S(1)}, bf16[256,128]{1,0:T(8,128)(2,1)}, u32[]{:S(2)}) copy-start(bf16[256,128]{1,0:T(8,128)(2,1)} %features.1) | copy-start | bytes 196612
  17.8 3.8 %copy-start.2 = (bf16[128,256]{1,0:T(8,128)(2,1)S(1)}, bf16[128,256]{1,0:T(8,128)(2,1)}, u32[]{:S(2)}) copy-start(bf16[128,256]{1,0:T(8,128)(2,1)} %w_hidden.1) | copy-start | bytes 196612

commit v2 on v1

--- a/solution.py
+++ b/solution.py
@@ -17,6 +17,7 @@
 HALF = 16
 LANES = 128
 PEER = CAP * HALF
+SPREAD = 32
 GROUP = 8
 
 F32 = jnp.float32
@@ -73,11 +74,15 @@
     features,
     w_hidden,
     w_out,
-    tiles,
+    values,
     request,
     code,
     prop_out,
     grad_out,
+    values_here,
+    by_entry,
+    by_row,
+    tiles,
     head_send,
     stat_send,
     stat_recv,
@@ -141,6 +146,9 @@
     def col_at(shift):
         return lax.rem(my_col + shift, cols)
 
+    to_vmem = pltpu.make_async_copy(values, values_here, local_sem.at[1])
+    to_vmem.start()
+
     barrier = pltpu.get_barrier_semaphore()
 
     def greet_dom(k, carry):
@@ -211,7 +219,21 @@
         inverse[r] = 1.0 / (1.0 + jnp.concatenate([sums, sums], axis=1))
         return carry
 
-    lax.fori_loop(0, row_blocks, degree, 0, unroll=4)
+    def rearrange(group, carry):
+        rows = BLOCK * BLOCK // LANES
+        first = pl.multiple_of(group * SPREAD, SPREAD)
+        for m in range(rows):
+            part = values_here[pl.ds(first, SPREAD), m * LANES : (m + 1) * LANES]
+            by_entry[pl.ds(m, SPREAD, stride=rows), :] = part.astype(F32)
+        left = lax.broadcasted_iota(jnp.int32, (rows, LANES), 1) < BLOCK
+        for pair in range(SPREAD // 2):
+            one = by_entry[2 * pair * rows : (2 * pair + 1) * rows, :]
+            two = by_entry[(2 * pair + 1) * rows : (2 * pair + 2) * rows, :]
+            by_row[pl.ds(pair * BLOCK, rows, stride=2), :] = jnp.where(left, one, swap(two))
+            by_row[pl.ds(pair * BLOCK + 1, rows, stride=2), :] = jnp.where(left, swap(one), two)
+        for pair in range(SPREAD // 2):
+            tiles[group * (SPREAD // 2) + pair] = by_row[pair * BLOCK : (pair + 1) * BLOCK, :].astype(BF16)
+        return carry
 
     def all_requests(wait):
         whole = pltpu.make_async_remote_copy(
@@ -323,10 +345,13 @@
 
         lax.fori_loop(0, peers, send, 0)
         if step == 0:
+            to_vmem.wait()
+            lax.fori_loop(0, entries // SPREAD, rearrange, 0)
+            lax.fori_loop(0, row_blocks, degree, 0, unroll=4)
+        elif step == 1:
             lax.fori_loop(0, chunks // 2, build_local, 0)
-        elif step == 1:
+        else:
             lax.fori_loop(0, peers, build_remote, 0)
-        else:
             lax.fori_loop(0, doms // 2, build_route, 0)
             acc[chunks] = jnp.zeros((HALF, LANES), F32)
             for late in range(STEPS):
@@ -559,9 +584,7 @@
     share = w_out.shape[1] // cols
     entries = block_slot.shape[0]
     index, chunks = index_tables(block_slot, doms, row_blocks)
-    tiles = (
-        block_values.reshape(entries // 2, 2, BLOCK, BLOCK).transpose(0, 2, 1, 3).reshape(entries // 2, BLOCK, LANES)
-    )
+    rows = BLOCK * BLOCK // LANES
     asked = jnp.where(requested < 0, row_blocks, requested)
     request = jnp.broadcast_to(asked.reshape(doms, 1, 1, CAP, 1), (doms, 1, 2, CAP, HALF)).reshape(doms, 1, LANES)
     code = (labels + 256 * train_mask).reshape(row_blocks, 1, 1, BLOCK)
@@ -575,9 +598,13 @@
     return pl.pallas_call(
         functools.partial(kernel, doms, cols, NCLASS, chunks),
         out_shape=[jax.ShapeDtypeStruct((share, nodes), F32)] * 2,
-        in_specs=[pl.BlockSpec(memory_space=pltpu.SMEM)] + [in_vmem] * 6,
+        in_specs=[pl.BlockSpec(memory_space=pltpu.SMEM)] + [in_vmem] * 3 + [pl.BlockSpec(memory_space=pl.ANY)] + [in_vmem] * 2,
         out_specs=[in_vmem] * 2,
         scratch_shapes=[
+            vmem((entries, BLOCK * BLOCK), BF16),
+            vmem((SPREAD * rows, LANES), F32),
+            vmem((SPREAD * rows, LANES), F32),
+            vmem((entries // 2, BLOCK, LANES), BF16),
             vmem((cols * mine, HALF, LANES), BF16),
             vmem((row_blocks, LANES), F32),
             vmem((cols - 1, row_blocks, LANES), F32),
@@ -605,14 +632,14 @@
             dma((2, cols - 1)),
             dma((2, cols - 1)),
             dma((2,)),
-            dma((1,)),
+            dma((2,)),
             dma((2 * STEPS,)),
             dma((2 * STEPS,)),
         ],
         compiler_params=pltpu.CompilerParams(
             collective_id=0, has_side_effects=True, vmem_limit_bytes=48 * 2**20
         ),
-    )(index, features, w_hidden, w_out, tiles, request, code)
+    )(index, features, w_hidden, w_out, block_values, request, code)
 
 
 def solution(mesh):

time: 147 us -> 136 us (0.925)
  local copies, waits for them, and re-layouts: 18.4 us -> 5.85 us
    reshape x2 -> x0, local copies, waits for them, and re-layouts: 10.3 us -> none  [body(): block_values.reshape(entries // 2, 2, BLOCK, BLOCK).transpose(0, 2, 1, 3)]
    transpose x1 -> x0, local copies, waits for them, and re-layouts: 6.47 us -> none  [body(): block_values.reshape(entries // 2, 2, BLOCK, BLOCK).transpose(0, 2, 1, 3)]
    unnamed x14 -> x10, local copies, waits for them, and re-layouts: 1.43 us -> 5.6 us
where the time goes in v2:
time: 136 us
  Pallas kernels  124 us (91%)
  local copies, waits for them, and re-layouts  5.85 us (4%)
  other arithmetic  5.16 us (4%)
    pallas_call x1, Pallas kernels, body(): pl.pallas_call(functools.partial(kernel, doms, cols, NCLASS, chunks), out...  124 us
    unnamed x10, local copies, waits for them, and re-layouts  5.6 us

profile of v2, /device:TPU:1, one launch (start us, length us, event | category | flops | bytes accessed | tf_op | source)
XLA Modules:
  0.0 135.6 jit_solution(2773227072081278689)
XLA Ops:
  0.6 0.8 convert_reduce_fusion.1
  1.4 0.1 select_reduce_fusion.3
  1.6 0.8 select_reduce_fusion.2
  2.3 0.1 convert_reduce_fusion.2
  2.4 0.9 convert_reduce_fusion
  3.4 0.7 fusion.2
  4.1 0.7 multiply_add_fusion
  4.8 0.1 broadcast_in_dim.113
  4.8 0.7 add_select_fusion
  5.6 0.1 select_reduce_fusion
  5.7 0.1 select_reduce_fusion.1
  6.0 0.1 broadcast_in_dim.115.code
  6.1 0.1 copy.12.request
  6.1 0.0 copy-start
  6.1 1.6 %copy-done = bf16[256,4096]{1,0:T(8,128)(2,1)S(1)} copy-done((bf16[256,4096]{1,0:T(8,128)(2,1)S(1)}, bf16[256,4096]{1,0:T(8,128)(2,1)}, u32[]{:S(2)}) %copy-start) | copy-done | bytes 2097176
  7.7 0.0 copy-start.1
  7.7 0.9 copy-done.1
  8.6 0.0 copy-start.2
  8.6 0.8 copy-done.2
  9.5 0.0 copy-start.3
  9.5 0.8 copy-done.3
  10.3 123.9 %shard_map.95 = (f32[32,2048]{1,0:T(8,128)S(1)}, f32[32,2048]{1,0:T(8,128)S(1)}) custom-call(s32[1568]{0:T(1024)S(1)} %constant_dynamic-update-slice_fusion.index, bf16[256,128]{1,0:T(8,128)(2,1)S(1)} %copy-done.2, bf16[128,256]{1,0:T(8,128)(2,1)S(1)} %copy-done.3, bf16[256,256]{1,0:T(8,128)(2,1)S(1)} %copy-done.1, bf16[256,4096]{1,0:T(8,128)(2,1)S(1)} %copy-done, ...), custom_call_target="tpu_custom_call" | custom-call | tf_op jit(solution)/shard_map/pallas_call | solution.py:598
  134.2 0.7 copy.24
  134.9 0.7 copy.25
  (13 shorter events, 0.1 us)
Async XLA Ops:
  6.1 1.6 %copy-start = (bf16[256,4096]{1,0:T(8,128)(2,1)S(1)}, bf16[256,4096]{1,0:T(8,128)(2,1)}, u32[]{:S(2)}) copy-start(bf16[256,4096]{1,0:T(8,128)(2,1)} %values.1) | copy-start | bytes 6291460
  7.7 0.9 copy-start.1
  8.6 0.8 copy-start.2
  9.5 0.8 copy-start.3
